TPU v7x, 128 devices: a whole 4x4x4 slice. The times are simulated.
128 devices in a mesh: section: 4 (over x), dp: 32 (over y, z, core).
Axes of the slice: x: 4, y: 4, z: 4, core: 2. Of those that a mesh axis runs over, the one named last changes fastest.
Arguments:
- bottom_stack_feed: bfloat16 [64, 64, 1024], P('dp'), may hold values from -6 to 6
- loss_sensitivity: bfloat16 [64, 64, 1024], P('dp'), may hold values from -6 to 6
- resumes_segment: int32 [64], P('dp'), may hold values 0 or 1
- mixing_coefficients: float32 [4, 9, 1024], P('section'), may hold values from -0.9 to 1.45, as said below
- fading_log: float32 [4, 1024], P('section'), may hold values from -6 to -3
- feature_boost: float32 [4, 1024], P('section'), may hold values from -1 to 1
- attention_maps: bfloat16 [4, 3, 1024, 1024], P('section'), may hold values from -0.1875 to 0.1875
- emission_coefficients: bfloat16 [4, 1024, 1024], P('section'), may hold values from -0.75 to 0.75
- feature_addressing: bfloat16 [4, 1024, 4096], P('section'), may hold values from -0.1875 to 0.1875
- feature_payload: bfloat16 [4, 4096, 1024], P('section'), may hold values from -0.09375 to 0.09375
- feature_receptance: bfloat16 [4, 1024, 1024], P('section'), may hold values from -0.1875 to 0.1875
- dividend_memory: float32 [4, 64, 1024], P('section', 'dp'), may hold values from -6 to 6
- divisor_memory: float32 [4, 64, 1024], P('section', 'dp'), may hold values from 0.5 to 4
- memory_power_shift: float32 [4, 64, 1024], P('section', 'dp'), may hold values from -1 to 1
- prior_normed_lines: bfloat16 [4, 2, 64, 1024], P('section', None, 'dp'), may hold values from -6 to 6
Outputs:
- layer_outputs: bfloat16 [4, 64, 64, 1024], P('section', 'dp')
- input_grads: bfloat16 [4, 64, 64, 1024], P('section', 'dp')
- vector_grads: float32 [4, 9, 1024], P('section', None, 'dp')
- decay_grads: float32 [4, 1024], P('section', 'dp')
- bonus_grads: float32 [4, 1024], P('section', 'dp')
- projection_grads: float32 [4, 3, 1024, 1024], P('section', None, 'dp')
- out_weight_grads: float32 [4, 1024, 1024], P('section', 'dp')
- ffn_key_grads: float32 [4, 1024, 4096], P('section', 'dp')
- ffn_value_grads: float32 [4, 4096, 1024], P('section', 'dp')
- ffn_gate_grads: float32 [4, 1024, 1024], P('section', 'dp')
- state_num_grads: float32 [4, 64, 1024], P('section', 'dp')
- state_den_grads: float32 [4, 64, 1024], P('section', 'dp')
- state_max_grads: float32 [4, 64, 1024], P('section', 'dp')
- earlier_row_grads: float32 [4, 2, 64, 1024], P('section', None, 'dp')
Inputs may be any that keep to these rules, and one draw needn't show every extreme that they name: `resumes_segment`: 1 where a sequence continues an earlier segment whose states and last normed rows are given, 0 where it starts afresh. `mixing_coefficients`: rows 0 and 5 are gains near 1, rows 1 and 6 biases, rows 2, 3, 4, 7 and 8 mixing weights within 0.05 to 0.95.
All inputs are finite; a program needn't handle non-finite values. No bound on the sum of `resumes_segment` on one device may be relied on, other than what follows from the above.
Results may differ from a plain program's by a relative error of at most 0.038.
Values may be sent and summed in bfloat16 or wider, within the bound.
No kernel may reach another device: no remote copies, remote signals or barrier semaphores. Data moves between devices by JAX's collectives and lax.ppermute only.
A program may use at most 256 MiB of HBM per device.

v0:
```python
import jax
import jax.numpy as jnp
from jax import lax
from jax.sharding import PartitionSpec as P

BLOCK = 64


FRESH = -1e30
HIGH = lax.Precision.HIGHEST


def passed_along(block, axis, distance):
    devices = range(lax.axis_size(axis))
    route = [(i - distance, i) for i in devices if i - distance in devices]
    return lax.ppermute(block, axis, route)


def norm_mix(rows, gain, offset, mixings, first_row):
    center = jnp.mean(rows, axis=-1, keepdims=True)
    centered = rows - center
    variance = jnp.mean(centered * centered, axis=-1, keepdims=True)
    normed = centered * lax.rsqrt(variance + 1e-05) * gain + offset
    shifted = jnp.concatenate([first_row[None, :], normed[:-1]], axis=0)
    return tuple((normed * mixing + shifted * (1.0 - mixing) for mixing in mixings))


def weighted_value_blocks(
    addressing_lines,
    payload_lines,
    fading_factor_log,
    position_boost,
    initial_numerator,
    initial_weight,
    initial_level,
):
    length, width = addressing_lines.shape
    blocks = length // BLOCK
    fading_factor = jnp.exp(fading_factor_log)
    offsets = lax.iota(jnp.float32, BLOCK)[:, None]
    lower = (lax.iota(jnp.int32, BLOCK)[None, :] < lax.iota(jnp.int32, BLOCK)[:, None]).astype(
        jnp.float32
    )

    def advance(carry, pieces):
        dividend_amount, accumulated_coefficient, shift_amount = carry
        addressing_groups, block_values = pieces
        peak = jnp.max(addressing_groups, axis=0)
        common_shift = jnp.maximum(shift_amount, peak)
        weighted = jnp.exp(addressing_groups - peak + offsets * fading_factor)
        summed = jnp.dot(
            lower, weighted * block_values, precision=HIGH, preferred_element_type=jnp.float32
        )
        counted = jnp.dot(lower, weighted, precision=HIGH, preferred_element_type=jnp.float32)
        from_state = jnp.exp(shift_amount - common_shift - offsets * fading_factor)
        from_block = jnp.exp(peak - common_shift - (offsets - 1.0) * fading_factor)
        diagonal_contribution = jnp.exp(position_boost + addressing_groups - common_shift)
        numerator = (
            from_state * dividend_amount
            + from_block * summed
            + diagonal_contribution * block_values
        )
        denominator = (
            from_state * accumulated_coefficient + from_block * counted + diagonal_contribution
        )
        fade = jnp.exp(shift_amount - common_shift - BLOCK * fading_factor)
        tail = jnp.exp(peak - common_shift - (BLOCK - 1) * fading_factor)
        new_number = fade * dividend_amount + tail * jnp.sum(weighted * block_values, axis=0)
        new_weight = fade * accumulated_coefficient + tail * jnp.sum(weighted, axis=0)
        return ((new_number, new_weight, common_shift), numerator / denominator)

    _, results = lax.scan(
        advance,
        (initial_numerator, initial_weight, initial_level),
        (
            addressing_lines.reshape(blocks, BLOCK, width),
            payload_lines.reshape(blocks, BLOCK, width),
        ),
    )
    return results.reshape(length, width)


def temporal_core(
    addressing_lines,
    payload_lines,
    gate_rows,
    fading_factor_log,
    position_boost,
    dividend_amount,
    accumulated_coefficient,
    shift_amount,
    toggle_marker,
):
    initial_level = jnp.where(toggle_marker > 0.0, shift_amount, FRESH)
    blended_lines = weighted_value_blocks(
        addressing_lines,
        payload_lines,
        fading_factor_log,
        position_boost,
        toggle_marker * dividend_amount,
        toggle_marker * accumulated_coefficient,
        initial_level,
    )
    return jax.nn.sigmoid(gate_rows) * blended_lines


def transposed(left, right):
    return lax.dot_general(
        left, right, (((0,), (0,)), ((), ())), preferred_element_type=jnp.float32
    )


def against(grad, weight):
    return lax.dot_general(
        grad, weight, (((1,), (1,)), ((), ())), preferred_element_type=jnp.float32
    )


def forward_layer(element_amount, parameters, states, toggle_marker):
    (
        direction_array,
        fading_factor_log,
        position_boost,
        affine_map,
        emission_map,
        addressing_map,
        payload_map,
        receptance_map,
    ) = parameters
    dividend_amount, accumulated_coefficient, shift_amount, position_before = states
    residual = element_amount.astype(jnp.float32)
    first = norm_mix(
        residual,
        direction_array[0],
        direction_array[1],
        (direction_array[2], direction_array[3], direction_array[4]),
        toggle_marker * position_before[0],
    )
    mix_key, mix_value, mix_gate = [piece.astype(jnp.bfloat16) for piece in first]
    addressing_lines = jnp.dot(mix_key, affine_map[0], preferred_element_type=jnp.float32)
    payload_lines = jnp.dot(mix_value, affine_map[1], preferred_element_type=jnp.float32)
    gate_rows = jnp.dot(mix_gate, affine_map[2], preferred_element_type=jnp.float32)
    recurrent_core = temporal_core(
        addressing_lines,
        payload_lines,
        gate_rows,
        fading_factor_log,
        position_boost,
        dividend_amount,
        accumulated_coefficient,
        shift_amount,
        toggle_marker,
    ).astype(jnp.bfloat16)
    middle = residual + jnp.dot(recurrent_core, emission_map, preferred_element_type=jnp.float32)
    second = norm_mix(
        middle,
        direction_array[5],
        direction_array[6],
        (direction_array[7], direction_array[8]),
        toggle_marker * position_before[1],
    )
    mix_hidden, mix_outer = [piece.astype(jnp.bfloat16) for piece in second]
    hidden_pre = jnp.dot(mix_hidden, addressing_map, preferred_element_type=jnp.float32)
    hidden = jnp.square(jax.nn.relu(hidden_pre)).astype(jnp.bfloat16)
    channel = jnp.dot(hidden, payload_map, preferred_element_type=jnp.float32)
    outer_pre = jnp.dot(mix_outer, receptance_map, preferred_element_type=jnp.float32)
    result = (middle + jax.nn.sigmoid(outer_pre) * channel).astype(jnp.bfloat16)
    saved = (
        mix_key,
        mix_value,
        mix_gate,
        addressing_lines,
        payload_lines,
        gate_rows,
        recurrent_core,
        middle,
        mix_hidden,
        mix_outer,
        hidden_pre,
        hidden,
        channel,
        outer_pre,
    )
    return (result, saved)


def backward_layer(element_amount, saved, grad_out, parameters, states, toggle_marker):
    (
        direction_array,
        fading_factor_log,
        position_boost,
        affine_map,
        emission_map,
        addressing_map,
        payload_map,
        receptance_map,
    ) = parameters
    dividend_amount, accumulated_coefficient, shift_amount, position_before = states
    (
        mix_key,
        mix_value,
        mix_gate,
        addressing_lines,
        payload_lines,
        gate_rows,
        recurrent_core,
        middle,
        mix_hidden,
        mix_outer,
        hidden_pre,
        hidden,
        channel,
        outer_pre,
    ) = saved
    residual = element_amount.astype(jnp.float32)
    sigma = jax.nn.sigmoid(outer_pre)
    grad_channel = (grad_out * sigma).astype(jnp.bfloat16)
    grad_outer = (grad_out * channel * sigma * (1.0 - sigma)).astype(jnp.bfloat16)
    grad_hidden = against(grad_channel, payload_map)
    grad_hidden_pre = (grad_hidden * 2.0 * jax.nn.relu(hidden_pre)).astype(jnp.bfloat16)
    key_proj_grad = transposed(mix_hidden, grad_hidden_pre)
    value_proj_grad = transposed(hidden, grad_channel)
    gate_proj_grad = transposed(mix_outer, grad_outer)

    def second_mix(rows, gain, offset, mix_one, mix_two, row_two):
        return norm_mix(rows, gain, offset, (mix_one, mix_two), toggle_marker * row_two)

    _, pull_second = jax.vjp(
        second_mix,
        middle,
        direction_array[5],
        direction_array[6],
        direction_array[7],
        direction_array[8],
        position_before[1],
    )
    middle_part, gain_two_grad, offset_two_grad, hidden_mix_grad, outer_mix_grad, row_two_grad = (
        pull_second((against(grad_hidden_pre, addressing_map), against(grad_outer, receptance_map)))
    )
    grad_middle = grad_out + middle_part
    grad_branch = grad_middle.astype(jnp.bfloat16)
    out_proj_grad = transposed(recurrent_core, grad_branch)
    grad_core = against(grad_branch, emission_map)

    def local_core(
        addressing_lines,
        payload_lines,
        gate_rows,
        fading_factor_log,
        position_boost,
        dividend_amount,
        accumulated_coefficient,
        shift_amount,
    ):
        return temporal_core(
            addressing_lines,
            payload_lines,
            gate_rows,
            fading_factor_log,
            position_boost,
            dividend_amount,
            accumulated_coefficient,
            shift_amount,
            toggle_marker,
        )

    _, pull_core = jax.vjp(
        local_core,
        addressing_lines,
        payload_lines,
        gate_rows,
        fading_factor_log,
        position_boost,
        dividend_amount,
        accumulated_coefficient,
        shift_amount,
    )
    (
        keys_grad,
        values_grad,
        gates_grad,
        rate_grad,
        boost_adjoint,
        number_grad,
        weight_grad,
        level_grad,
    ) = pull_core(grad_core)
    keys_grad = keys_grad.astype(jnp.bfloat16)
    values_grad = values_grad.astype(jnp.bfloat16)
    gates_grad = gates_grad.astype(jnp.bfloat16)
    projection_grad = jnp.stack(
        [
            transposed(mix_key, keys_grad),
            transposed(mix_value, values_grad),
            transposed(mix_gate, gates_grad),
        ]
    )

    def first_mix(rows, gain, offset, mix_one, mix_two, mix_three, row_one):
        return norm_mix(rows, gain, offset, (mix_one, mix_two, mix_three), toggle_marker * row_one)

    _, pull_first = jax.vjp(
        first_mix,
        residual,
        direction_array[0],
        direction_array[1],
        direction_array[2],
        direction_array[3],
        direction_array[4],
        position_before[0],
    )
    (
        residual_part,
        gain_one_grad,
        offset_one_grad,
        key_mix_grad,
        value_mix_grad,
        gate_mix_grad,
        row_one_grad,
    ) = pull_first(
        (
            against(keys_grad, affine_map[0]),
            against(values_grad, affine_map[1]),
            against(gates_grad, affine_map[2]),
        )
    )
    grad_entry = (grad_middle + residual_part).astype(jnp.bfloat16)
    vector_grad = jnp.stack(
        [
            gain_one_grad,
            offset_one_grad,
            key_mix_grad,
            value_mix_grad,
            gate_mix_grad,
            gain_two_grad,
            offset_two_grad,
            hidden_mix_grad,
            outer_mix_grad,
        ]
    )
    weight_grads = (
        vector_grad,
        rate_grad,
        boost_adjoint,
        projection_grad,
        out_proj_grad,
        key_proj_grad,
        value_proj_grad,
        gate_proj_grad,
    )
    return (
        grad_entry,
        weight_grads,
        (number_grad, weight_grad, level_grad),
        jnp.stack([row_one_grad, row_two_grad]),
    )


def body(
    bottom_stack_feed,
    loss_sensitivity,
    resumes_segment,
    mixing_coefficients,
    fading_log,
    feature_boost,
    attention_maps,
    emission_coefficients,
    feature_addressing,
    feature_payload,
    feature_receptance,
    dividend_memory,
    divisor_memory,
    memory_power_shift,
    prior_normed_lines,
):
    micro, length, width = bottom_stack_feed.shape
    inner = feature_addressing.shape[2]
    sections = lax.axis_size("section")
    section = lax.axis_index("section")
    ticks = micro + sections - 1
    parameters = (
        mixing_coefficients[0],
        fading_log[0],
        feature_boost[0],
        attention_maps[0],
        emission_coefficients[0],
        feature_addressing[0],
        feature_payload[0],
        feature_receptance[0],
    )

    def states_of(slot):
        return (
            lax.dynamic_index_in_dim(dividend_memory[0], slot, 0, keepdims=False),
            lax.dynamic_index_in_dim(divisor_memory[0], slot, 0, keepdims=False),
            lax.dynamic_index_in_dim(memory_power_shift[0], slot, 0, keepdims=False),
            lax.dynamic_index_in_dim(prior_normed_lines[0], slot, 1, keepdims=False).astype(
                jnp.float32
            ),
        )

    def flag_of(slot):
        return lax.dynamic_index_in_dim(resumes_segment, slot, 0, keepdims=False).astype(
            jnp.float32
        )

    stored = ()
    entries = jnp.zeros((micro, length, width), jnp.bfloat16)
    emitted_lines = jnp.zeros((micro, length, width), jnp.bfloat16)
    incoming = jnp.zeros((length, width), jnp.bfloat16)
    for tick in range(ticks):
        position_number = tick - section
        slot = jnp.clip(position_number, 0, micro - 1)
        active = (position_number >= 0) & (position_number < micro)
        element_amount = jnp.where(
            section == 0,
            lax.dynamic_index_in_dim(bottom_stack_feed, slot, 0, keepdims=False),
            incoming,
        )

        def run_forward(carry, element_amount=element_amount, slot=slot):
            entries_now, outputs_now, stored_now = carry
            result, saved = forward_layer(
                element_amount, parameters, states_of(slot), flag_of(slot)
            )
            entries_now = lax.dynamic_update_index_in_dim(entries_now, element_amount, slot, 0)
            outputs_now = lax.dynamic_update_index_in_dim(outputs_now, result, slot, 0)
            stored_now = tuple(
                (
                    lax.dynamic_update_index_in_dim(buffer, piece, slot, 0)
                    for buffer, piece in zip(stored_now, saved)
                )
            )
            return (result, (entries_now, outputs_now, stored_now))

        def skip_forward(carry):
            return (jnp.zeros((length, width), jnp.bfloat16), carry)

        result, (entries, emitted_lines, stored) = lax.cond(
            active, run_forward, skip_forward, (entries, emitted_lines, stored)
        )
        if tick + 1 < ticks:
            incoming = passed_along(result, "section", 1)
    summed = (
        jnp.zeros((9, width), jnp.float32),
        jnp.zeros((width,), jnp.float32),
        jnp.zeros((width,), jnp.float32),
        jnp.zeros((3, width, width), jnp.float32),
        jnp.zeros((width, width), jnp.float32),
        jnp.zeros((width, inner), jnp.float32),
        jnp.zeros((inner, width), jnp.float32),
        jnp.zeros((width, width), jnp.float32),
    )
    shards = None
    grad_inputs = jnp.zeros((micro, length, width), jnp.bfloat16)
    state_grads = tuple((jnp.zeros((micro, width), jnp.float32) for _ in range(3)))
    row_grads = jnp.zeros((2, micro, width), jnp.float32)
    arriving = jnp.zeros((length, width), jnp.bfloat16)
    for tick in range(ticks):
        position_number = tick - (sections - 1 - section)
        slot = jnp.clip(position_number, 0, micro - 1)
        active = (position_number >= 0) & (position_number < micro)
        grad_out = jnp.where(
            section == sections - 1,
            lax.dynamic_index_in_dim(loss_sensitivity, slot, 0, keepdims=False),
            arriving,
        ).astype(jnp.float32)

        def run_backward(carry, grad_out=grad_out, slot=slot):
            summed_now, inputs_now, states_now, rows_now = carry
            element_amount = lax.dynamic_index_in_dim(entries, slot, 0, keepdims=False)
            saved = forward_layer(element_amount, parameters, states_of(slot), flag_of(slot))[1]
            grad_entry, weight_grads, state_parts, row_parts = backward_layer(
                element_amount, saved, grad_out, parameters, states_of(slot), flag_of(slot)
            )
            summed_now = tuple((total + piece for total, piece in zip(summed_now, weight_grads)))
            inputs_now = lax.dynamic_update_index_in_dim(inputs_now, grad_entry, slot, 0)
            states_now = tuple(
                (
                    lax.dynamic_update_index_in_dim(buffer, piece, slot, 0)
                    for buffer, piece in zip(states_now, state_parts)
                )
            )
            rows_now = lax.dynamic_update_index_in_dim(rows_now, row_parts, slot, 1)
            return (grad_entry, (summed_now, inputs_now, states_now, rows_now))

        def skip_backward(carry):
            return (jnp.zeros((length, width), jnp.bfloat16), carry)

        grad_entry, (summed, grad_inputs, state_grads, row_grads) = lax.cond(
            active, run_backward, skip_backward, (summed, grad_inputs, state_grads, row_grads)
        )
        if tick + 1 < ticks:
            arriving = passed_along(grad_entry, "section", -1)
    shards = (
        lax.psum_scatter(
            summed[0].astype(jnp.bfloat16), "dp", scatter_dimension=1, tiled=True
        ).astype(jnp.float32),
        lax.psum_scatter(
            summed[1].astype(jnp.bfloat16), "dp", scatter_dimension=0, tiled=True
        ).astype(jnp.float32),
        lax.psum_scatter(
            summed[2].astype(jnp.bfloat16), "dp", scatter_dimension=0, tiled=True
        ).astype(jnp.float32),
        lax.psum_scatter(
            summed[3].astype(jnp.bfloat16), "dp", scatter_dimension=1, tiled=True
        ).astype(jnp.float32),
        lax.psum_scatter(
            summed[4].astype(jnp.bfloat16), "dp", scatter_dimension=0, tiled=True
        ).astype(jnp.float32),
        lax.psum_scatter(
            summed[5].astype(jnp.bfloat16), "dp", scatter_dimension=0, tiled=True
        ).astype(jnp.float32),
        lax.psum_scatter(
            summed[6].astype(jnp.bfloat16), "dp", scatter_dimension=0, tiled=True
        ).astype(jnp.float32),
        lax.psum_scatter(
            summed[7].astype(jnp.bfloat16), "dp", scatter_dimension=0, tiled=True
        ).astype(jnp.float32),
    )
    return (
        emitted_lines[None],
        grad_inputs[None],
        shards[0][None],
        shards[1][None],
        shards[2][None],
        shards[3][None],
        shards[4][None],
        shards[5][None],
        shards[6][None],
        shards[7][None],
        state_grads[0][None],
        state_grads[1][None],
        state_grads[2][None],
        row_grads[None],
    )


def solution(mesh):
    placed = (
        P("dp", None, None),
        P("dp", None, None),
        P("dp"),
        P("section", None, None),
        P("section", None),
        P("section", None),
        P("section", None, None, None),
        P("section", None, None),
        P("section", None, None),
        P("section", None, None),
        P("section", None, None),
        P("section", "dp", None),
        P("section", "dp", None),
        P("section", "dp", None),
        P("section", None, "dp", None),
    )
    return jax.shard_map(
        body,
        mesh=mesh,
        in_specs=placed,
        out_specs=(
            P("section", "dp", None, None),
            P("section", "dp", None, None),
            P("section", None, "dp"),
            P("section", "dp"),
            P("section", "dp"),
            P("section", None, "dp", None),
            P("section", "dp", None),
            P("section", "dp", None),
            P("section", "dp", None),
            P("section", "dp", None),
            P("section", "dp", None),
            P("section", "dp", None),
            P("section", "dp", None),
            P("section", None, "dp", None),
        ),
        check_vma=False,
    )
```

profile of v0, /device:TPU:0, one launch (start us, length us, event | category | flops | bytes accessed | tf_op | source)
XLA Modules:
  0.0 1206.8 jit_solution(10921937794372317944)
XLA Ops:
  8.0 27.3 %conditional.10 = (bf16[64,1024]{1,0:T(8,128)(2,1)S(1)}, bf16[2,64,1024]{2,1,0:T(8,128)(2,1)S(1)}, bf16[2,64,1024]{2,1,0:T(8,128)(2,1)}) conditional(s32[]{:T(128)} %convert_element_type.774, () %tuple.155, (pred[]{:T(512)}, f32[9,1024]{1,0:T(8,128)S(1)}, s32[]{:T(128)}, s32[2]{0:T(128)}, bf16[1,2,2,1024]{3,2,1,0:T(2,128)(2,1)}, ...), branch_computations={%region_0.1_spmd, %region_1.7_spmd.clone.clone} | conditional | flops 1853577472 | bytes 55149716 | solution.py:439
  14.6 2.9 fusion.1008
  24.3 9.0 fusion.480
  37.3 2.8 collective-permute-done
  40.1 26.7 %conditional.11 = (bf16[64,1024]{1,0:T(8,128)(2,1)}, bf16[2,64,1024]{2,1,0:T(8,128)(2,1)S(1)}, bf16[2,64,1024]{2,1,0:T(8,128)(2,1)}) conditional(s32[]{:T(128)} %convert_element_type.773, (bf16[2,64,1024]{2,1,0:T(8,128)(2,1)S(1)}, bf16[2,64,1024]{2,1,0:T(8,128)(2,1)}) %tuple.157, (pred[]{:T(512)}, f32[9,1024]{1,0:T(8,128)S(1)}, ...), branch_computations={%region_7.8_spmd, %region_8.14_spmd.clone.clone} | conditional | flops 1853577472 | bytes 52528216 | solution.py:439
  46.7 2.9 fusion.1013
  56.4 9.0 fusion.565
  66.8 4.2 collective-permute-start.1
  71.0 2.8 collective-permute-done.1
  74.5 30.1 %collective-permute-start.2 = (bf16[64,1024]{1,0:T(8,128)(2,1)}, bf16[64,1024]{1,0:T(8,128)(2,1)S(1)}, u32[]{:S(2)}, u32[]{:S(2)}) collective-permute-start(bf16[64,1024]{1,0:T(8,128)(2,1)} %get-tuple-element.2561), channel_id=1, source_target_pairs={{0,32},{32,64},{64,96},{1,33},{33,65},{65,97},{2,34},{34,66},{66,9... | collective-permute-start | bytes 393224 | tf_op jit(solution)/shard_map/ppermute | solution.py:16
  104.6 2.8 collective-permute-done.2
  108.2 4.3 collective-permute-start.3
  115.3 40.3 %conditional.15 = (bf16[64,1024]{1,0:T(8,128)(2,1)}, f32[9,1024]{1,0:T(8,128)S(1)}, f32[1024]{0:T(1024)}, f32[1024]{0:T(1024)S(1)}, f32[3,1024,1024]{2,1,0:T(8,1...) conditional(s32[]{:T(128)} %convert_element_type.779, ...), branch_computations={%region_35.36_spmd, %region_36.72_spmd.clone.clone} | conditional | flops 5464604672 | bytes 266630576 | solution.py:490
  115.7 7.8 broadcast_in_dim.1050
  123.5 7.9 broadcast_in_dim.1051
  131.4 6.1 broadcast_in_dim.1049
  156.9 29.6 %collective-permute-done.4 = bf16[64,1024]{1,0:T(8,128)(2,1)S(1)} collective-permute-done((bf16[64,1024]{1,0:T(8,128)(2,1)}, bf16[64,1024]{1,0:T(8,128)(2,1)S(1)}, u32[]{:S(2)}, u32[]{:S(2)}) %collective-permute-start.4) | collective-permute-done | bytes 131104 | tf_op jit(solution)/shard_map/ppermute | solution.py:16
  187.4 9.0 conditional.16
  197.7 5.9 collective-permute-done.5
  204.5 9.0 conditional.17
  214.8 254.6 %collective-permute-done.6 = bf16[64,1024]{1,0:T(8,128)(2,1)S(1)} collective-permute-done((bf16[64,1024]{1,0:T(8,128)(2,1)S(1)}, bf16[64,1024]{1,0:T(8,128)(2,1)S(1)}, u32[]{:S(2)}, u32[]{:S(2)}) %collective-permute-start.6) | collective-permute-done | bytes 131104 | tf_op jit(solution)/shard_map/ppermute | solution.py:16
  470.3 99.3 %conditional.18 = (bf16[64,1024]{1,0:T(8,128)(2,1)S(1)}, f32[9,1024]{1,0:T(8,128)S(1)}, f32[1024]{0:T(1024)}, f32[1024]{0:T(1024)S(1)}, f32[3,1024,1024]{2,1,0:T...) conditional(s32[]{:T(128)} %convert_element_type.776, ...), branch_computations={%region_146.147_spmd, %region_147.183_spmd} | conditional | flops 5477657600 | bytes 316844096 | solution.py:490
  478.8 2.8 fusion.1001
  489.5 5.1 convolution_maximum_fusion.2
  511.6 11.6 maximum_add_fusion.2
  523.2 14.0 %convolution_add_fusion.13 = f32[1024,4096]{1,0:T(8,128)} fusion(f32[1024,4096]{1,0:T(8,128)} %get-tuple-element.2406, bf16[64,1024]{1,0:T(8,128)(2,1)S(1)} %get-tuple-element.3634, bf16[64,4096]{1,0:T(8,128)(2,1)S(1)} %fusion.219), kind=kOutput, calls=%fused_computation.420 | convolution fusion | flops 541065216 | bytes 34209792 | tf_op jit(solution)/shard_map/cond/branch_1_fun/dot_general | solution.py:108
  537.2 13.9 %convolution_add_fusion.12 = f32[4096,1024]{1,0:T(8,128)} fusion(f32[4096,1024]{1,0:T(8,128)} %get-tuple-element.2407, bf16[64,1024]{1,0:T(8,128)(2,1)S(1)} %get-tuple-element.3669, f32[64,4096]{1,0:T(8,128)S(1)} %convolution_maximum_fusion.2), kind=kOutput, calls=%fused_computation.419 | convolution fusion | flops 541589504 | bytes 34734080 | tf_op jit(solution)/shard_map/cond/branch_1_fun/dot_general | solution.py:108
  554.0 4.9 convolution_add_fusion.15
  558.9 5.0 convolution_add_fusion.14
  571.0 5.6 collective-permute-done.7
  577.5 97.0 %conditional.19 = (f32[9,1024]{1,0:T(8,128)S(1)}, f32[1024]{0:T(1024)}, f32[1024]{0:T(1024)S(1)}, f32[3,1024,1024]{2,1,0:T(8,128)}, f32[1024,1024]{1,0:T(8,128)}...) conditional(s32[]{:T(128)} %convert_element_type.775, ...), branch_computations={%region_183.184_spmd, %region_184.220_spmd} | conditional | flops 5477657600 | bytes 314531424 | solution.py:490
  594.3 5.3 convolution_maximum_fusion.3
  619.5 11.2 maximum_add_fusion.3
  630.6 13.9 %convolution_add_fusion.19 = f32[1024,4096]{1,0:T(8,128)} fusion(f32[1024,4096]{1,0:T(8,128)} %get-tuple-element.2448, bf16[64,1024]{1,0:T(8,128)(2,1)S(1)} %get-tuple-element.3683, bf16[64,4096]{1,0:T(8,128)(2,1)S(1)} %fusion.328), kind=kOutput, calls=%fused_computation.629 | convolution fusion | flops 541065216 | bytes 34209792 | tf_op jit(solution)/shard_map/cond/branch_1_fun/dot_general | solution.py:108
  644.5 13.9 %convolution_add_fusion.18 = f32[4096,1024]{1,0:T(8,128)} fusion(f32[4096,1024]{1,0:T(8,128)} %get-tuple-element.2449, bf16[64,1024]{1,0:T(8,128)(2,1)S(1)} %get-tuple-element.3718, f32[64,4096]{1,0:T(8,128)S(1)} %convolution_maximum_fusion.3), kind=kOutput, calls=%fused_computation.628 | convolution fusion | flops 541589504 | bytes 34734080 | tf_op jit(solution)/shard_map/cond/branch_1_fun/dot_general | solution.py:108
  660.3 4.9 convolution_add_fusion.21
  665.2 5.0 convolution_add_fusion.20
  675.5 3.8 convert_element_type.793
  679.4 3.9 convert_element_type.790
  683.3 8.3 convert_element_type.789
  691.7 9.2 convert_element_type.792
  700.9 9.1 convert_element_type.791
  712.6 64.4 %all-reduce.12 = (bf16[1024]{0:T(1024)(128)(2,1)S(1)}, bf16[1024]{0:T(1024)(128)(2,1)S(1)}) all-reduce(bf16[1024]{0:T(1024)(128)(2,1)S(1)} %convert_element_type.787, bf16[1024]{0:T(1024)(128)(2,1)S(1)} %convert_element_type.788), channel_id=3, replica_groups=mesh['section'=4,'dp'=32] {'dp'}, use_global_device_ids=true, to_apply=%region_221.222.clone | all-reduce | flops 2048 | bytes 8192
  779.0 56.0 %reduce-scatter.17.cloned.1.call-done = bf16[32,1024]{1,0:T(8,128)(2,1)} async-done(((bf16[1024,1024]{1,0:T(8,128)(2,1)}), bf16[32,1024]{1,0:T(8,128)(2,1)}) %reduce-scatter.17.cloned.1.call-update) | async-done | bytes 65552 | tf_op jit(solution)/shard_map/reduce_scatter | solution.py:517
  836.5 80.4 %reduce-scatter.11.cloned.1.call-done = bf16[32,1024]{1,0:T(8,128)(2,1)} async-done(((bf16[1024,1024]{1,0:T(8,128)(2,1)}), bf16[32,1024]{1,0:T(8,128)(2,1)}) %reduce-scatter.11.cloned.1.call-update) | async-done | bytes 65552 | tf_op jit(solution)/shard_map/reduce_scatter | solution.py:508
  918.3 87.8 %reduce-scatter.9.cloned.1.call-done = bf16[3,32,1024]{2,1,0:T(8,128)(2,1)} async-done(((bf16[3,1024,1024]{2,1,0:T(8,128)(2,1)}), bf16[3,32,1024]{2,1,0:T(8,128)(2,1)}) %reduce-scatter.9.cloned.1.call-update) | async-done | bytes 196624 | tf_op jit(solution)/shard_map/reduce_scatter | solution.py:505
  1007.9 94.3 %reduce-scatter.15.cloned.1.call-done = bf16[128,1024]{1,0:T(8,128)(2,1)} async-done(((bf16[4096,1024]{1,0:T(8,128)(2,1)}), bf16[128,1024]{1,0:T(8,128)(2,1)}) %reduce-scatter.15.cloned.1.call-update) | async-done | bytes 262160 | tf_op jit(solution)/shard_map/reduce_scatter | solution.py:514
  1104.0 93.9 %reduce-scatter.13.cloned.1.call-done = bf16[32,4096]{1,0:T(8,128)(2,1)} async-done(((bf16[1024,4096]{1,0:T(8,128)(2,1)}), bf16[32,4096]{1,0:T(8,128)(2,1)}) %reduce-scatter.13.cloned.1.call-update) | async-done | bytes 262160 | tf_op jit(solution)/shard_map/reduce_scatter | solution.py:511
  (439 shorter events, 150.4 us)
Async XLA Ops:
  7.2 770.4 %reduce-scatter.19.cloned.1.call-start = ((), (), s32[]{:S(2)}) async-start(), calls=%async_computation.11 | async-start | bytes 270336
  8.1 9.4 copy-start.59
  8.1 9.4 copy-start.66
  8.1 9.4 copy-start.37
  8.1 9.4 copy-start.80
  8.1 10.9 copy-start.52
  8.1 13.2 %copy-start = (bf16[1024,1024]{1,0:T(8,128)(2,1)S(1)}, bf16[1024,1024]{1,0:T(8,128)(2,1)}, u32[]{:S(2)}) copy-start(bf16[1024,1024]{1,0:T(8,128)(2,1)} %get-tuple-element.2987) | copy-start | bytes 6291460 | tf_op jit(solution)/shard_map/cond
  9.3 14.7 %copy-start.10 = (bf16[2,64,1024]{2,1,0:T(8,128)(2,1)}, bf16[2,64,1024]{2,1,0:T(8,128)(2,1)S(1)}, u32[]{:S(2)}) copy-start(bf16[2,64,1024]{2,1,0:T(8,128)(2,1)S(1)} %get-tuple-element.3899) | copy-start | bytes 786436 | tf_op jit(solution)/shard_map/cond
  24.3 9.8 copy-start.12
  24.3 11.0 copy-start.11
  36.0 4.1 collective-permute-start
  40.2 9.3 copy-start.60
  40.2 9.3 copy-start.67
  40.3 9.4 copy-start.38
  40.3 9.4 copy-start.81
  40.3 10.9 copy-start.53
  40.3 13.1 %copy-start.1 = (bf16[1024,1024]{1,0:T(8,128)(2,1)S(1)}, bf16[1024,1024]{1,0:T(8,128)(2,1)}, u32[]{:S(2)}) copy-start(bf16[1024,1024]{1,0:T(8,128)(2,1)} %get-tuple-element.3025) | copy-start | bytes 6291460 | tf_op jit(solution)/shard_map/cond
  56.4 9.0 copy-start.13
  66.8 7.1 collective-permute-start.1
  74.5 32.9 %collective-permute-start.2 = (bf16[64,1024]{1,0:T(8,128)(2,1)}, bf16[64,1024]{1,0:T(8,128)(2,1)S(1)}, u32[]{:S(2)}, u32[]{:S(2)}) collective-permute-start(bf16[64,1024]{1,0:T(8,128)(2,1)} %get-tuple-element.2561), channel_id=1, source_target_pairs={{0,32},{32,64},{64,96},{1,33},{33,65},{65,97},{2,34},{34,66},{66,9... | collective-permute-start | bytes 393224 | tf_op jit(solution)/shard_map/ppermute | solution.py:16
  108.2 7.1 collective-permute-start.3
  155.6 30.9 %collective-permute-start.4 = (bf16[64,1024]{1,0:T(8,128)(2,1)}, bf16[64,1024]{1,0:T(8,128)(2,1)S(1)}, u32[]{:S(2)}, u32[]{:S(2)}) collective-permute-start(bf16[64,1024]{1,0:T(8,128)(2,1)} %get-tuple-element.2580), channel_id=1, source_target_pairs={{32,0},{64,32},{96,64},{33,1},{65,33},{97,65},{34,2},{66,34},{98,6... | collective-permute-start | bytes 393224 | tf_op jit(solution)/shard_map/ppermute | solution.py:16
  196.4 7.2 collective-permute-start.5
  213.5 255.9 %collective-permute-start.6 = (bf16[64,1024]{1,0:T(8,128)(2,1)S(1)}, bf16[64,1024]{1,0:T(8,128)(2,1)S(1)}, u32[]{:S(2)}, u32[]{:S(2)}) collective-permute-start(bf16[64,1024]{1,0:T(8,128)(2,1)S(1)} %get-tuple-element.2608), channel_id=1, source_target_pairs={{32,0},{64,32},{96,64},{33,1},{65,33},{97,65},{34,2},{66,34},{98,6... | collective-permute-start | bytes 393224 | tf_op jit(solution)/shard_map/ppermute | solution.py:16
  470.4 12.1 %copy-start.45 = (f32[1024]{0:T(1024)S(1)}, f32[1024]{0:T(1024)}, u32[]{:S(2)}) copy-start(f32[1024]{0:T(1024)} %get-tuple-element.2393) | copy-start | bytes 12292 | tf_op jit(solution)/shard_map/cond
  471.0 10.6 copy-start.175
  471.7 9.9 copy-start.189
  472.3 9.3 copy-start.116
  472.4 9.3 copy-start.118
  476.5 11.9 copy-start.8
  478.8 10.2 copy-start.28
  481.7 7.6 copy-start.124
  511.6 39.5 %slice-start.26 = ((s8[6291456]{0:T(1024)(128)(4,1)}), s8[4194304]{0:T(1024)(128)(4,1)S(1)}, s32[]{:S(2)}) async-start(s8[6291456]{0:T(1024)(128)(4,1)} %bitcast.1505), calls=%async_computation.38 | async-start | bytes 8388608 | tf_op jit(solution)/shard_map/cond
  523.2 27.9 %slice-start.27 = ((s8[6291456]{0:T(1024)(128)(4,1)}), s8[2097152]{0:T(1024)(128)(4,1)S(1)}, s32[]{:S(2)}) async-start(s8[6291456]{0:T(1024)(128)(4,1)} %bitcast.1505), calls=%async_computation.39 | async-start | bytes 4194304 | tf_op jit(solution)/shard_map/cond
  569.7 6.9 collective-permute-start.7
  577.5 10.8 copy-start.65
  577.5 10.8 copy-start.72
  577.5 10.9 copy-start.46
  577.5 11.6 copy-start.58
  577.6 11.6 copy-start.89
  578.3 7.8 copy-start.178
  579.1 9.2 copy-start.192
  583.8 7.8 copy-start.9
  675.4 159.5 %reduce-scatter.17.cloned.1.call-start = ((), (), s32[]{:S(2)}) async-start(), calls=%async_computation.10 | async-start | bytes 2162688 | tf_op jit(solution)/shard_map/reduce_scatter | solution.py:517
  679.3 237.5 %reduce-scatter.11.cloned.1.call-start = ((), (), s32[]{:S(2)}) async-start(), calls=%async_computation.7 | async-start | bytes 2162688 | tf_op jit(solution)/shard_map/reduce_scatter | solution.py:508
  683.3 322.9 %reduce-scatter.9.cloned.1.call-start = ((), (), s32[]{:S(2)}) async-start(), calls=%async_computation.6 | async-start | bytes 6488064 | tf_op jit(solution)/shard_map/reduce_scatter | solution.py:505
  691.6 410.6 %reduce-scatter.15.cloned.1.call-start = ((), (), s32[]{:S(2)}) async-start(), calls=%async_computation.9 | async-start | bytes 8650752 | tf_op jit(solution)/shard_map/reduce_scatter | solution.py:514
  700.8 497.1 %reduce-scatter.13.cloned.1.call-start = ((), (), s32[]{:S(2)}) async-start(), calls=%async_computation.8 | async-start | bytes 8650752 | tf_op jit(solution)/shard_map/reduce_scatter | solution.py:511
  (60 other events, 283.6 us)
Sparse Core Ops, SparseCore 0:
  675.5 77.6 reduce-scatter.18
  756.7 78.1 reduce-scatter.16
  838.5 78.2 reduce-scatter.10
  920.4 85.7 reduce-scatter.8
  1010.2 91.9 reduce-scatter.14
  1105.8 92.0 reduce-scatter.12
where the time goes:
time: 1210 us
  waiting for transfers between devices  719 us (59%)
  matrix products  178 us (15%)
  other arithmetic  95.8 us (8%)
  blocking collectives  64.4 us (5%)
  local copies, waits for them, and re-layouts  56.3 us (5%)
  starting transfers between devices  45.2 us (4%)
  loops' own time  32.2 us (3%)
  between operations  15.3 us (1%)
    ppermute x8, waiting for transfers between devices, passed_along(): return lax.ppermute(block, axis, route)  307 us
    reduce_scatter x1, waiting for transfers between devices, body(): lax.psum_scatter(summed[6].astype(jnp.bfloat16), 'dp', scatter_dimension=...  94.3 us
    reduce_scatter x1, waiting for transfers between devices, body(): lax.psum_scatter(summed[5].astype(jnp.bfloat16), 'dp', scatter_dimension=...  93.9 us
    reduce_scatter x1, waiting for transfers between devices, body(): lax.psum_scatter(summed[3].astype(jnp.bfloat16), 'dp', scatter_dimension=...  87.8 us
    reduce_scatter x1, waiting for transfers between devices, body(): lax.psum_scatter(summed[4].astype(jnp.bfloat16), 'dp', scatter_dimension=...  80.4 us
    dot_general x14, matrix products, transposed(): lax.dot_general(left, right, (((0,), (0,)), ((), ())), preferred_element_...  80.1 us
    unnamed x1, blocking collectives  64.4 us
    reduce_scatter x1, waiting for transfers between devices, body(): lax.psum_scatter(summed[7].astype(jnp.bfloat16), 'dp', scatter_dimension=...  56 us
  transfers between devices with their start and end apart: 14, of which 13 were waited for; matrix products, arithmetic and copies ran while one was open for 4% of the time, Pallas kernels for 0%

commit v1 on v0

v1 whole, which is shorter than its diff:
```python
import functools

import jax
import jax.numpy as jnp
from jax import lax
from jax.experimental import pallas as pl
from jax.experimental.pallas import tpu as pltpu
from jax.sharding import PartitionSpec as P

WIDTH = 1024
INNER = 4096
LENGTH = 64
SEQS = 2
ROWS = SEQS * LENGTH
GROUPS = WIDTH // 128
FRESH = -1e30
EPS = 1e-05
F32 = jnp.float32
BF16 = jnp.bfloat16

VM = pl.BlockSpec(memory_space=pltpu.VMEM)
HB = pl.BlockSpec(memory_space=pl.ANY)
SM = pl.BlockSpec(memory_space=pltpu.SMEM)
PARAMS = pltpu.CompilerParams(vmem_limit_bytes=18 * 1024 * 1024)

WEIGHTS = (
    ((3, WIDTH, WIDTH), BF16),
    ((WIDTH, WIDTH), BF16),
    ((WIDTH, INNER), BF16),
    ((INNER, WIDTH), BF16),
    ((WIDTH, WIDTH), BF16),
)
SAVED = (
    ((ROWS, WIDTH), BF16),
    ((ROWS, WIDTH), BF16),
    ((6, ROWS, WIDTH), BF16),
    ((ROWS, INNER), BF16),
    ((ROWS, INNER), BF16),
    ((5, ROWS, WIDTH), F32),
    ((8, ROWS * GROUPS, 128), F32),
)
GRADS = (
    ((ROWS, WIDTH), BF16),
    ((6, ROWS, WIDTH), BF16),
    ((ROWS, INNER), BF16),
    ((16, WIDTH), F32),
    ((3, SEQS, WIDTH), F32),
    ((2, SEQS, WIDTH), F32),
)


def dot(left, right):
    return jnp.dot(left, right, preferred_element_type=F32)


def against(grad, weight):
    return lax.dot_general(
        grad, weight, (((1,), (1,)), ((), ())), preferred_element_type=F32
    )


def row_index():
    return lax.broadcasted_iota(jnp.int32, (ROWS, WIDTH), 0)


def normed_rows(rows):
    center = jnp.mean(rows, axis=-1, keepdims=True)
    centered = rows - center
    variance = jnp.mean(centered * centered, axis=-1, keepdims=True)
    scale = lax.rsqrt(variance + EPS)
    return centered * scale, scale


def moved_down(normed, first):
    index = row_index()
    return jnp.where(
        index == 0,
        first[0],
        jnp.where(index == LENGTH, first[1], pltpu.roll(normed, 1, 0)),
    )


def moved_up(rows):
    index = row_index()
    return jnp.where(
        (index == LENGTH - 1) | (index == ROWS - 1),
        0.0,
        pltpu.roll(rows, ROWS - 1, 0),
    )


def first_rows(prior_ref, mix, marks):
    return [prior_ref[mix, s : s + 1, :].astype(F32) * marks[s] for s in range(SEQS)]


def to_tokens(ref, block, value):
    ref[pl.ds(block, ROWS, stride=GROUPS), :] = value


def from_tokens(ref, block):
    return ref[pl.ds(block, ROWS, stride=GROUPS), :]


def tile_of(ref, row, small):
    for g in range(GROUPS):
        small[g : g + 1, :] = ref[row : row + 1, g * 128 : (g + 1) * 128]
    return small[...]


def forward_body(
    marks, x_ref, vec_ref, fade_ref, boost_ref, num_ref, den_ref, lev_ref, prior_ref,
    weights, ready, out_ref, saved, scratch,
):
    wm, wo, wa, wp, wr = weights
    ent_ref, lay_ref, mix_ref, hid_ref, act_ref, wide_ref, scan_ref = saved
    sk, sv, sy, small = scratch
    x = x_ref[...]
    ent_ref[...] = x
    rows = x.astype(F32)
    unit, _ = normed_rows(rows)
    normed = unit * vec_ref[0:1, :] + vec_ref[1:2, :]
    below = moved_down(normed, first_rows(prior_ref, 0, marks))
    for j in range(3):
        v = vec_ref[2 + j : 3 + j, :]
        mix_ref[j] = (normed * v + below * (1.0 - v)).astype(BF16)
    ready(0)
    for target, j in ((sk, 0), (sv, 1)):
        for c in range(0, WIDTH, 256):
            part = dot(mix_ref[j], wm[j, :, c : c + 256])
            for h in range(2):
                to_tokens(target, c // 128 + h, part[:, h * 128 : (h + 1) * 128])
    wide_ref[0] = jax.nn.sigmoid(dot(mix_ref[2], wm[2]))

    rate = jnp.exp(tile_of(fade_ref, 0, small))
    boost = tile_of(boost_ref, 0, small)
    start = []
    for s in range(SEQS):
        level = tile_of(lev_ref, s, small)
        start.append(jnp.where(marks[s] > 0.0, level, FRESH))
        start.append(tile_of(num_ref, s, small) * marks[s])
        start.append(tile_of(den_ref, s, small) * marks[s])

    def token(t, carry):
        carry_next = []
        for s in range(SEQS):
            level, num, den = carry[3 * s : 3 * s + 3]
            at = pl.ds(pl.multiple_of((t + LENGTH * s) * GROUPS, GROUPS), GROUPS)
            key, value = sk[at, :], sv[at, :]
            boosted = boost + key
            decayed = jnp.exp(-jnp.abs(level - boosted))
            state_on_top = level > boosted
            old = jnp.where(state_on_top, 1.0, decayed)
            fresh = jnp.where(state_on_top, decayed, 1.0)
            inverse = 1.0 / (old * den + fresh)
            old = old * inverse
            fresh = fresh * inverse
            result = old * num + fresh * value
            faded = level - rate
            level = jnp.maximum(faded, key)
            decayed = jnp.exp(-jnp.abs(faded - key))
            state_on_top = faded > key
            keep = jnp.where(state_on_top, 1.0, decayed)
            new = jnp.where(state_on_top, decayed, 1.0)
            sy[at, :] = result
            scan_ref[0, at, :] = old
            scan_ref[1, at, :] = fresh
            scan_ref[2, at, :] = value - result
            scan_ref[3, at, :] = keep
            scan_ref[4, at, :] = new
            scan_ref[5, at, :] = num
            scan_ref[6, at, :] = den
            scan_ref[7, at, :] = value
            carry_next += [level, keep * num + new * value, keep * den + new]
        return tuple(carry_next)

    def tokens(block, carry):
        for j in range(8):
            carry = token(block * 8 + j, carry)
        return carry

    lax.fori_loop(0, LENGTH // 8, tokens, tuple(start))
    for g in range(GROUPS):
        at = slice(g * 128, (g + 1) * 128)
        gate = wide_ref[0, :, at]
        mixed = gate * from_tokens(sy, g)
        mix_ref[3, :, at] = mixed.astype(BF16)
        wide_ref[1, :, at] = mixed * (1.0 - gate)
    ready(1)
    wide_ref[2] = rows + dot(mix_ref[3], wo[...])
    unit, _ = normed_rows(wide_ref[2])
    normed = unit * vec_ref[5:6, :] + vec_ref[6:7, :]
    below = moved_down(normed, first_rows(prior_ref, 1, marks))
    for j in range(2):
        v = vec_ref[7 + j : 8 + j, :]
        mix_ref[4 + j] = (normed * v + below * (1.0 - v)).astype(BF16)
    ready(4)
    wide_ref[4] = jax.nn.sigmoid(dot(mix_ref[5], wr[...]))
    ready(2)

    @pl.loop(0, INNER // 512)
    def _(j):
        at = pl.ds(pl.multiple_of(j * 512, 512), 512)
        active = jnp.maximum(dot(mix_ref[4], wa[:, at]), 0.0)
        act_ref[:, at] = active.astype(BF16)
        hid_ref[:, at] = (active * active).astype(BF16)

    ready(3)

    @pl.loop(0, WIDTH // 256)
    def _(j):
        at = pl.ds(pl.multiple_of(j * 256, 256), 256)
        channel = dot(hid_ref[...], wp[:, at])
        wide_ref[3, :, at] = channel
        lay_ref[:, at] = (wide_ref[2, :, at] + wide_ref[4, :, at] * channel).astype(BF16)

    out_ref[...] = lay_ref[...]


N_SMALL = 8


def forward_first_kernel(flag, begins, x_ref, *refs):
    small_in = refs[: N_SMALL - 1]
    hbm = refs[N_SMALL - 1 : N_SMALL + 4]
    out_ref = refs[N_SMALL + 4]
    kept = refs[N_SMALL + 5 : N_SMALL + 10]
    saved = refs[N_SMALL + 10 : N_SMALL + 17]
    scratch = refs[N_SMALL + 17 : N_SMALL + 21]
    sem = refs[N_SMALL + 21]
    copies = [pltpu.make_async_copy(hbm[i], kept[i], sem.at[i]) for i in range(5)]
    for i in (0, 1, 4, 2, 3):
        copies[i].start()

    @pl.when(flag[0] == 1)
    def _():
        marks = [begins[s].astype(F32) for s in range(SEQS)]
        forward_body(
            marks, x_ref, *small_in, kept, lambda i: copies[i].wait(), out_ref, saved, scratch
        )

    @pl.when(flag[0] == 0)
    def _():
        for c in copies:
            c.wait()


def forward_kernel(flag, begins, x_ref, *refs):
    small_in = refs[: N_SMALL - 1]
    n = N_SMALL - 1 + 12
    out_ref = refs[n]
    kept = refs[n + 1 : n + 6]
    saved = refs[n + 6 : n + 13]
    scratch = refs[n + 13 :]

    @pl.when(flag[0] == 1)
    def _():
        marks = [begins[s].astype(F32) for s in range(SEQS)]
        forward_body(
            marks, x_ref, *small_in, kept, lambda i: None, out_ref, saved, scratch
        )


def norm_back(rows, gain, offset, first, parts, vec_out, prior_out, marks):
    unit, scale = normed_rows(rows)
    normed = unit * gain + offset
    change = normed - moved_down(normed, first)
    up, stay = None, None
    for grad, weight, place in parts:
        vec_out(place, jnp.sum(grad * change, axis=0, keepdims=True))
        kept = grad * weight
        passed = grad - kept
        stay = kept if stay is None else stay + kept
        up = passed if up is None else up + passed
    for s in range(SEQS):
        prior_out(s, up[s * LENGTH : s * LENGTH + 1, :] * marks[s])
    grad = stay + moved_up(up)
    return unit, scale, grad


def backward_kernel(first, flag, begins, dy_ref, *refs):
    vec_ref, fade_ref, prior_ref = refs[:3]
    n = 3 + 12 + (0 if first else 6)
    out_ref = refs[n]
    wm, wo, wa, wp, wr = refs[n + 1 : n + 6]
    ent_ref, lay_ref, mix_ref, hid_ref, act_ref, wide_ref, scan_ref = refs[n + 6 : n + 13]
    ing_ref, dys_ref, dhp_ref, vecg_ref, stg_ref, rowg_ref = refs[n + 13 : n + 19]
    sg, sdk, sdv, small, wide, wide_two, wide_three = refs[n + 19 :]

    def vec_out(place, value):
        vecg_ref[place : place + 1, :] = value

    @pl.when(flag[0] == 1)
    def _():
        marks = [begins[s].astype(F32) for s in range(SEQS)]
        dy = dy_ref[...].astype(F32)
        gate = wide_ref[4]
        through = dy * gate
        dys_ref[4] = through.astype(BF16)
        dys_ref[5] = (through * wide_ref[3] * (1.0 - gate)).astype(BF16)

        @pl.loop(0, INNER // 512)
        def _(j):
            at = pl.ds(pl.multiple_of(j * 512, 512), 512)
            part = against(dys_ref[4], wp[at, :])
            dhp_ref[:, at] = (2.0 * act_ref[:, at].astype(F32) * part).astype(BF16)

        @pl.loop(0, WIDTH // 256)
        def _(j):
            at = pl.ds(pl.multiple_of(j * 256, 256), 256)
            wide[:, at] = against(dhp_ref[...], wa[at, :])
            wide_two[:, at] = against(dys_ref[5], wr[at, :])

        def prior_two(s, value):
            rowg_ref[1, s : s + 1, :] = value

        gain = vec_ref[5:6, :]
        unit, scale, grad = norm_back(
            wide_ref[2], gain, vec_ref[6:7, :], first_rows(prior_ref, 1, marks),
            ((wide[...], vec_ref[7:8, :], 7), (wide_two[...], vec_ref[8:9, :], 8)),
            vec_out, prior_two, marks,
        )
        vec_out(5, jnp.sum(grad * unit, axis=0, keepdims=True))
        vec_out(6, jnp.sum(grad, axis=0, keepdims=True))
        grad = grad * gain
        mean = jnp.mean(grad, axis=-1, keepdims=True)
        along = jnp.mean(grad * unit, axis=-1, keepdims=True)
        middle = dy_ref[...].astype(F32) + scale * (grad - mean - unit * along)
        wide_three[...] = middle
        dys_ref[3] = middle.astype(BF16)
        for c in range(0, WIDTH, 256):
            part = against(dys_ref[3], wo[c : c + 256, :])
            at = slice(c, c + 256)
            dys_ref[2, :, at] = (part * wide_ref[1, :, at]).astype(BF16)
            part = part * wide_ref[0, :, at]
            for h in range(2):
                to_tokens(sg, c // 128 + h, part[:, h * 128 : (h + 1) * 128])

        zero = jnp.zeros((GROUPS, 128), F32)

        def token(t, carry):
            carry_next = []
            boosted, faded = carry[4], carry[5]
            for s in range(SEQS):
                dnum, dden = carry[2 * s : 2 * s + 2]
                at = pl.ds(pl.multiple_of((t + LENGTH * s) * GROUPS, GROUPS), GROUPS)
                g = sg[at, :]
                value = scan_ref[7, at, :]
                beyond = scan_ref[2, at, :]
                keep = scan_ref[3, at, :]
                new = scan_ref[4, at, :]
                from_old = scan_ref[0, at, :] * g
                from_new = scan_ref[1, at, :] * g
                direct = from_new * beyond
                boosted = boosted + direct
                sdv[at, :] = from_new + new * dnum
                sdk[at, :] = direct + new * (dnum * value + dden)
                faded = faded - keep * (dnum * scan_ref[5, at, :] + dden * scan_ref[6, at, :])
                carry_next += [
                    from_old + keep * dnum,
                    keep * dden - from_old * (value - beyond),
                ]
            return tuple(carry_next) + (boosted, faded)

        def tokens(block, carry):
            for j in range(8):
                carry = token(LENGTH - 1 - block * 8 - j, carry)
            return carry

        ends = lax.fori_loop(0, LENGTH // 8, tokens, (zero,) * 6)

        def spread(put, value):
            small[...] = value
            for g in range(GROUPS):
                put(slice(g * 128, (g + 1) * 128), small[g : g + 1, :])

        for s in range(SEQS):
            dnum, dden = ends[2 * s : 2 * s + 2]
            at = pl.ds(LENGTH * s * GROUPS, GROUPS)
            moved = dnum * scan_ref[5, at, :] + dden * scan_ref[6, at, :]
            for k, value in enumerate((dnum, dden, moved)):

                def put(cols, piece, k=k, s=s):
                    stg_ref[k, s : s + 1, cols] = piece

                spread(put, value * marks[s])

        def put_decay(cols, piece):
            vecg_ref[9:10, cols] = piece

        def put_boost(cols, piece):
            vecg_ref[10:11, cols] = piece

        spread(put_decay, ends[5])
        vecg_ref[9:10, :] = vecg_ref[9:10, :] * jnp.exp(fade_ref[0:1, :])
        spread(put_boost, ends[4])

        for g in range(GROUPS):
            at = slice(g * 128, (g + 1) * 128)
            dys_ref[0, :, at] = from_tokens(sdk, g).astype(BF16)
            dys_ref[1, :, at] = from_tokens(sdv, g).astype(BF16)

        rows = ent_ref[...].astype(F32)
        grads = [against(dys_ref[j], wm[j]) for j in range(3)]

        def prior_one(s, value):
            rowg_ref[0, s : s + 1, :] = value

        gain = vec_ref[0:1, :]
        unit, scale, grad = norm_back(
            rows, gain, vec_ref[1:2, :], first_rows(prior_ref, 0, marks),
            [(grads[j], vec_ref[2 + j : 3 + j, :], 2 + j) for j in range(3)],
            vec_out, prior_one, marks,
        )
        vec_out(0, jnp.sum(grad * unit, axis=0, keepdims=True))
        vec_out(1, jnp.sum(grad, axis=0, keepdims=True))
        grad = grad * gain
        mean = jnp.mean(grad, axis=-1, keepdims=True)
        along = jnp.mean(grad * unit, axis=-1, keepdims=True)
        entry = (wide_three[...] + scale * (grad - mean - unit * along)).astype(BF16)
        ing_ref[...] = entry
        out_ref[...] = entry


def plain(shapes):
    return tuple(jax.ShapeDtypeStruct(s, d) for s, d in shapes)


def in_vmem(shapes):
    return tuple(pltpu.VMEM(s, d) for s, d in shapes)


def hold(arrays):
    return tuple(pltpu.with_memory_space_constraint(a, pltpu.VMEM) for a in arrays)


ROWS_OUT = jax.ShapeDtypeStruct((ROWS, WIDTH), BF16)
TOKENS = pltpu.VMEM((ROWS * GROUPS, 128), F32)
SMALL = pltpu.VMEM((GROUPS, 128), F32)
WIDE = pltpu.VMEM((ROWS, WIDTH), F32)


def forward_first(flag, begins, rows, small, weights):
    results = pl.pallas_call(
        forward_first_kernel,
        out_shape=(ROWS_OUT,) + in_vmem(WEIGHTS) + in_vmem(SAVED),
        in_specs=[SM, SM] + [VM] * N_SMALL + [HB] * 5,
        out_specs=(VM,) * 13,
        scratch_shapes=[TOKENS, TOKENS, TOKENS, SMALL, pltpu.SemaphoreType.DMA((5,))],
        compiler_params=PARAMS,
    )(flag, begins, rows, *small, *weights)
    return results[0], results[1:6], results[6:]


def forward_next(flag, begins, rows, small, weights, saved):
    results = pl.pallas_call(
        forward_kernel,
        out_shape=(ROWS_OUT,) + plain(WEIGHTS) + plain(SAVED),
        in_specs=[SM, SM] + [VM] * (N_SMALL + 12),
        out_specs=(VM,) * 13,
        input_output_aliases={2 + N_SMALL + i: 1 + i for i in range(12)},
        scratch_shapes=[TOKENS, TOKENS, TOKENS, SMALL],
        compiler_params=PARAMS,
    )(flag, begins, rows, *small, *hold(weights), *hold(saved))
    return results[0], results[1:6], results[6:]


def backward_call(flag, begins, grad, small, weights, saved, grads):
    first = grads is None
    held = hold(weights) + hold(saved) + (() if first else hold(grads))
    results = pl.pallas_call(
        functools.partial(backward_kernel, first),
        out_shape=(ROWS_OUT,)
        + plain(WEIGHTS)
        + plain(SAVED)
        + (in_vmem(GRADS) if first else plain(GRADS)),
        in_specs=[SM, SM] + [VM] * (4 + len(held)),
        out_specs=(VM,) * 19,
        input_output_aliases={6 + i: 1 + i for i in range(len(held))},
        scratch_shapes=[TOKENS, TOKENS, TOKENS, SMALL, WIDE, WIDE, WIDE],
        compiler_params=PARAMS,
    )(flag, begins, grad, *small, *held)
    return results[0], results[1:6], results[6:13], results[13:]


def transposed(left, right):
    return lax.dot_general(
        left, right, (((0,), (0,)), ((), ())), preferred_element_type=F32
    ).astype(BF16)


def body(
    bottom_stack_feed,
    loss_sensitivity,
    resumes_segment,
    mixing_coefficients,
    fading_log,
    feature_boost,
    attention_maps,
    emission_coefficients,
    feature_addressing,
    feature_payload,
    feature_receptance,
    dividend_memory,
    divisor_memory,
    memory_power_shift,
    prior_normed_lines,
):
    sections = lax.axis_size("section")
    section = lax.axis_index("section")
    flags = [(section == t).astype(jnp.int32)[None] for t in range(sections)]
    small = (
        mixing_coefficients[0],
        fading_log,
        feature_boost,
        dividend_memory[0],
        divisor_memory[0],
        memory_power_shift[0],
        prior_normed_lines[0],
    )
    weights = (
        attention_maps[0],
        emission_coefficients[0],
        feature_addressing[0],
        feature_payload[0],
        feature_receptance[0],
    )
    rows, weights, saved = forward_first(
        flags[0], resumes_segment, bottom_stack_feed.reshape(ROWS, WIDTH), small, weights
    )
    for t in range(1, sections):
        rows = lax.ppermute(rows, "section", [(t - 1, t)])
        rows, weights, saved = forward_next(
            flags[t], resumes_segment, rows, small, weights, saved
        )
    back_small = (small[0], small[1], small[6])
    grad, weights, saved, grads = backward_call(
        flags[-1], resumes_segment, loss_sensitivity.reshape(ROWS, WIDTH), back_small,
        weights, saved, None,
    )
    for t in range(sections - 2, -1, -1):
        grad = lax.ppermute(grad, "section", [(t + 1, t)])
        grad, weights, saved, grads = backward_call(
            flags[t], resumes_segment, grad, back_small, weights, saved, grads
        )
    entry, layer, mixes, hidden, _, _, _ = saved
    entry_grad, outer, dhp, vecg, state_grads, row_grads = grads
    parts = [transposed(mixes[j], outer[j]) for j in range(4)]
    parts.append(transposed(mixes[4], dhp))
    parts.append(transposed(mixes[5], outer[5]))
    parts.append(jnp.pad(vecg.T, ((0, 0), (0, 112))).astype(BF16))
    payload = transposed(hidden, outer[4])
    shard = lax.psum_scatter(
        jnp.concatenate(parts, axis=1), "dp", scatter_dimension=0, tiled=True
    ).astype(F32)
    payload = lax.psum_scatter(payload, "dp", scatter_dimension=0, tiled=True).astype(F32)
    vectors = shard[:, 9 * WIDTH :].T
    return (
        layer.reshape(1, SEQS, LENGTH, WIDTH),
        entry_grad.reshape(1, SEQS, LENGTH, WIDTH),
        vectors[None, :9],
        vectors[9:10],
        vectors[10:11],
        jnp.stack([shard[:, j * WIDTH : (j + 1) * WIDTH] for j in range(3)])[None],
        shard[None, :, 3 * WIDTH : 4 * WIDTH],
        shard[None, :, 4 * WIDTH : 8 * WIDTH],
        payload[None],
        shard[None, :, 8 * WIDTH : 9 * WIDTH],
        state_grads[0][None],
        state_grads[1][None],
        state_grads[2][None],
        row_grads[None],
    )


def solution(mesh):
    placed = (
        P("dp", None, None),
        P("dp", None, None),
        P("dp"),
        P("section", None, None),
        P("section", None),
        P("section", None),
        P("section", None, None, None),
        P("section", None, None),
        P("section", None, None),
        P("section", None, None),
        P("section", None, None),
        P("section", "dp", None),
        P("section", "dp", None),
        P("section", "dp", None),
        P("section", None, "dp", None),
    )
    return jax.shard_map(
        body,
        mesh=mesh,
        in_specs=placed,
        out_specs=(
            P("section", "dp", None, None),
            P("section", "dp", None, None),
            P("section", None, "dp"),
            P("section", "dp"),
            P("section", "dp"),
            P("section", None, "dp", None),
            P("section", "dp", None),
            P("section", "dp", None),
            P("section", "dp", None),
            P("section", "dp", None),
            P("section", "dp", None),
            P("section", "dp", None),
            P("section", "dp", None),
            P("section", None, "dp", None),
        ),
        check_vma=False,
    )
```

time: 1210 us -> 518 us (0.43)
  waiting for transfers between devices: 719 us -> 267 us
  matrix products: 178 us -> 26.4 us
  local copies, waits for them, and re-layouts: 56.3 us -> 151 us
  other arithmetic: 95.8 us -> 3.72 us
  blocking collectives: 64.4 us -> 0 us
  Pallas kernels: 0 us -> 38.2 us
  starting transfers between devices: 45.2 us -> 7.51 us
  loops' own time: 32.2 us -> 0 us
    reduce_scatter x5 -> x2, waiting for transfers between devices: 412 us -> 167 us  [the longest x1 125 us: body(): lax.psum_scatter(jnp.concatenate(parts, axis=1), 'dp', scatter_dimension=...]
    ppermute x8 -> x6, waiting for transfers between devices: 307 us -> 99.8 us  [the longest x3 94 us: body(): grad = lax.ppermute(grad, 'section', [(t + 1, t)])]
    unnamed x9 -> x148, local copies, waits for them, and re-layouts: 4.9 us -> 132 us
    dot_general x50 -> x0, matrix products: 98 us -> none  [the longest x4 21.2 us: forward_layer(): channel = jnp.dot(hidden, payload_map, preferred_element_type=jnp.float32)]
    unnamed x1 -> x0, blocking collectives: 64.4 us -> none
    dot_general x14 -> x7, matrix products: 80.1 us -> 26.4 us  [transposed(): lax.dot_general(left, right, (((0,), (0,)), ((), ())), preferred_element_...]
    convert_element_type x20 -> x1, other arithmetic: 42.8 us -> 1.15 us  [body(): shard = lax.psum_scatter(jnp.concatenate(parts, axis=1), 'dp', scatter_di...]
    pallas_call x0 -> x8, Pallas kernels: none -> 38.2 us  [the longest x4 19.9 us: backward_call(): pl.pallas_call(functools.partial(backward_kernel, first), out_shape=(ROWS...]
  transfers between devices with their start and end apart: 14 -> 8, of which waited for: 13 -> 4; matrix products, arithmetic and copies ran while one was open for 4% -> 10% of each run, Pallas kernels for 0% -> 0%
where the time goes in v1:
time: 518 us; the launch traced here: 508 us
  waiting for transfers between devices  267 us (52%)
  local copies, waits for them, and re-layouts  151 us (29%)
  Pallas kernels  38.2 us (7%)
  matrix products  26.4 us (5%)
  between operations  14.8 us (3%)
  starting transfers between devices  7.51 us (1%)
    unnamed x148, local copies, waits for them, and re-layouts  132 us
    reduce_scatter x1, waiting for transfers between devices, body(): lax.psum_scatter(jnp.concatenate(parts, axis=1), 'dp', scatter_dimension=...  125 us
    ppermute x3, waiting for transfers between devices, body(): grad = lax.ppermute(grad, 'section', [(t + 1, t)])  94 us
    reduce_scatter x1, waiting for transfers between devices, body(): lax.psum_scatter(payload, 'dp', scatter_dimension=0, tiled=True).astype(F32)  42.5 us
    dot_general x7, matrix products, transposed(): lax.dot_general(left, right, (((0,), (0,)), ((), ())), preferred_element_...  26.4 us
    pallas_call x4, Pallas kernels, backward_call(): pl.pallas_call(functools.partial(backward_kernel, first), out_shape=(ROWS...  19.9 us
    convert_element_type x4, local copies, waits for them, and re-layouts, transposed(): return lax.dot_general(left, right, (((0,), (0,)), ((), ())), preferred_e...  16.1 us
    pallas_call x1, Pallas kernels, forward_first(): pl.pallas_call(forward_first_kernel, out_shape=(ROWS_OUT,) + in_vmem(WEIG...  12.8 us
  transfers between devices with their start and end apart: 8, of which 4 were waited for; matrix products, arithmetic and copies ran while one was open for 10% of the time, Pallas kernels for 0%

profile of v1, /device:TPU:0, one launch (start us, length us, event | category | flops | bytes accessed | tf_op | source)
XLA Modules:
  0.0 508.3 jit_solution(14291714872470449952)
XLA Ops:
  8.6 12.8 %shard_map.254 = (bf16[128,1024]{1,0:T(8,128)(2,1)}, bf16[3,1024,1024]{2,1,0:T(8,128)(2,1)S(1)}, bf16[1024,1024]{1,0:T(8,128)(2,1)S(1)}, bf16[1024,4096]{1,0:T(8...) custom-call(s32[1]{0:T(128)} %bitcast.flag, ...), custom_call_target="tpu_custom_call" | custom-call | tf_op jit(solution)/shard_map/pallas_call | solution.py:443
  21.5 3.4 copy-done
  24.8 3.3 copy-done.6
  28.1 2.6 copy-done.12
  30.8 2.0 copy-done.18
  40.0 5.8 %collective-permute-done.x_ref = bf16[128,1024]{1,0:T(8,128)(2,1)S(1)} collective-permute-done((bf16[128,1024]{1,0:T(8,128)(2,1)}, bf16[128,1024]{1,0:T(8,128)(2,1)S(1)}, u32[]{:S(2)}, u32[]{:S(2)}) %collective-permute-start) | collective-permute-done | bytes 262176 | tf_op jit(solution)/shard_map/ppermute | solution.py:531
  46.5 3.4 copy-done.1
  49.8 3.4 copy-done.7
  53.2 2.8 copy-done.13
  56.0 2.2 copy-done.19
  65.2 1.7 shard_map.255
  67.0 3.4 copy-done.2
  70.4 3.3 copy-done.8
  73.7 2.6 copy-done.14
  76.3 2.0 copy-done.20
  85.6 3.4 copy-done.3
  89.0 3.4 copy-done.9
  92.4 2.8 copy-done.15
  95.1 2.2 copy-done.21
  104.4 1.7 shard_map.256
  106.1 3.4 copy-done.4
  109.5 3.3 copy-done.10
  112.8 2.6 copy-done.16
  115.4 2.0 copy-done.22
  124.7 3.4 copy-done.5
  128.1 3.4 copy-done.11
  131.5 2.8 copy-done.17
  134.3 2.2 copy-done.23
  143.5 1.9 shard_map.257
  148.5 1.7 shard_map.259
  150.2 2.6 collective-permute-start.4
  156.6 94.0 %collective-permute-done.5.dy_ref = bf16[128,1024]{1,0:T(8,128)(2,1)S(1)} collective-permute-done((bf16[128,1024]{1,0:T(8,128)(2,1)}, bf16[128,1024]{1,0:T(8,128)(2,1)S(1)}, u32[]{:S(2)}, u32[]{:S(2)}) %collective-permute-start.5) | collective-permute-done | bytes 262176 | tf_op jit(solution)/shard_map/ppermute | solution.py:541
  251.2 14.8 %shard_map.261 = (bf16[128,1024]{1,0:T(8,128)(2,1)}, bf16[3,1024,1024]{2,1,0:T(8,128)(2,1)S(1)}, bf16[1024,1024]{1,0:T(8,128)(2,1)S(1)}, bf16[1024,4096]{1,0:T(8...) custom-call(s32[1]{0:T(128)} %bitcast.flag, ...), custom_call_target="tpu_custom_call", output_to_operand_aliasing={{1}: (6, {}), {2}: (7, {}), {3}: (8, {}), {4}: (9, {}), {5}... | custom-call | tf_op jit(solution)/shard_map/pallas_call | solution.py:470
  269.3 5.7 %convolution_convert_fusion = bf16[4096,1024]{1,0:T(8,128)(2,1)} fusion(bf16[128,4096]{1,0:T(8,128)(2,1)S(1)} %get-tuple-element.245, bf16[6,128,1024]{2,1,0:T(8,128)(2,1)S(1)} %get-tuple-element.242), kind=kOutput, calls=%fused_computation.1 | convolution fusion | flops 1077936128 | bytes 9699328 | tf_op jit(solution)/shard_map/dot_general | solution.py:486
  276.4 3.0 convolution_convert_fusion.1
  279.4 3.9 copy.135
  283.3 3.0 convolution_convert_fusion.2
  286.3 4.0 copy.134
  290.4 3.0 convolution_convert_fusion.3
  293.4 4.1 copy.133
  297.4 3.0 convolution_convert_fusion.4
  300.5 4.0 copy.132
  304.5 3.5 constant_dynamic-update-slice_fusion.3
  314.5 5.7 %convert_dynamic-update-slice_fusion = bf16[1024,9344]{1,0:T(8,128)(2,1)} fusion(bf16[1024,9344]{1,0:T(8,128)(2,1)} %constant_dynamic-update-slice_fusion, bf16[128,4096]{1,0:T(8,128)(2,1)S(1)} %copy-done.58, bf16[6,128,1024]{2,1,0:T(8,128)(2,1)S(1)} %copy-done.43), kind=kOutput, calls=%fused_computation | convolution fusion | flops 1077936128 | bytes 9699328 | tf_op jit(solution)/shard_map/dot_general | solution.py:486
  320.2 3.0 convert_dynamic-update-slice_fusion.1
  326.7 42.5 %reduce-scatter.5.cloned.1.call-done = bf16[128,1024]{1,0:T(8,128)(2,1)} async-done(((bf16[4096,1024]{1,0:T(8,128)(2,1)}), bf16[128,1024]{1,0:T(8,128)(2,1)}) %reduce-scatter.5.cloned.1.call-update) | async-done | bytes 262160 | tf_op jit(solution)/shard_map/reduce_scatter | solution.py:555
  369.2 1.8 bitcast_convert_fusion
  371.0 124.5 %reduce-scatter.3.cloned.1.call-done = bf16[32,9344]{1,0:T(8,128)(2,1)} async-done(((bf16[1024,9344]{1,0:T(8,128)(2,1)}), bf16[32,9344]{1,0:T(8,128)(2,1)}) %reduce-scatter.3.cloned.1.call-update) | async-done | bytes 598032 | tf_op jit(solution)/shard_map/reduce_scatter | solution.py:552
  (148 shorter events, 72.4 us)
Async XLA Ops:
  7.2 362.0 %reduce-scatter.5.cloned.1.call-start = ((), (), s32[]{:S(2)}) async-start(), calls=%async_computation.3 | async-start | bytes 8650752 | tf_op jit(solution)/shard_map/reduce_scatter | solution.py:555
  21.5 3.4 copy-start
  24.8 3.3 copy-start.6
  28.1 2.6 copy-start.12
  30.8 2.1 copy-start.18
  32.8 1.4 copy-start.24
  38.7 7.1 %collective-permute-start = (bf16[128,1024]{1,0:T(8,128)(2,1)}, bf16[128,1024]{1,0:T(8,128)(2,1)S(1)}, u32[]{:S(2)}, u32[]{:S(2)}) collective-permute-start(bf16[128,1024]{1,0:T(8,128)(2,1)} %get-tuple-element.131), channel_id=1, source_target_pairs={{0,32},{1,33},{2,34},{3,35},{4,36},{5,37},{6,38},{7,39},{8,40},{9,... | collective-permute-start | bytes 786440 | tf_op jit(solution)/shard_map/ppermute | solution.py:531
  46.5 3.4 copy-start.1
  49.8 3.4 copy-start.7
  53.2 2.8 copy-start.13
  56.0 2.2 copy-start.19
  58.2 1.6 copy-start.25
  59.8 1.6 copy-start.31
  61.4 1.4 copy-start.37
  67.0 3.4 copy-start.2
  70.4 3.3 copy-start.8
  73.7 2.6 copy-start.14
  76.3 2.1 copy-start.20
  78.4 1.4 copy-start.26
  84.2 0.7 collective-permute-start.1
  85.6 3.4 copy-start.3
  89.0 3.4 copy-start.9
  92.4 2.8 copy-start.15
  95.1 2.2 copy-start.21
  97.3 1.6 copy-start.27
  98.9 1.6 copy-start.33
  100.5 1.4 copy-start.39
  106.1 3.4 copy-start.4
  109.5 3.3 copy-start.10
  112.8 2.6 copy-start.16
  115.4 2.1 copy-start.22
  117.5 1.4 copy-start.28
  123.3 0.7 collective-permute-start.2
  124.7 3.4 copy-start.5
  128.1 3.4 copy-start.11
  131.5 2.8 copy-start.17
  134.3 2.2 copy-start.23
  136.5 1.6 copy-start.29
  138.1 1.6 copy-start.35
  147.1 0.7 collective-permute-start.3
  150.2 2.6 collective-permute-start.4
  155.3 95.2 %collective-permute-start.5 = (bf16[128,1024]{1,0:T(8,128)(2,1)}, bf16[128,1024]{1,0:T(8,128)(2,1)S(1)}, u32[]{:S(2)}, u32[]{:S(2)}) collective-permute-start(bf16[128,1024]{1,0:T(8,128)(2,1)} %get-tuple-element.220), channel_id=1, source_target_pairs={{32,0},{33,1},{34,2},{35,3},{36,4},{37,5},{38,6},{39,7},{40,8},{41... | collective-permute-start | bytes 786440 | tf_op jit(solution)/shard_map/ppermute | solution.py:541
  275.0 1.4 copy-start.43
  275.0 220.5 %reduce-scatter.3.cloned.1.call-start = ((), (), s32[]{:S(2)}) async-start(), calls=%async_computation.2 | async-start | bytes 19734528 | tf_op jit(solution)/shard_map/reduce_scatter | solution.py:552
  304.5 3.5 copy-start.61
  308.0 2.5 copy-start.60
  310.4 2.5 copy-start.59
  312.9 1.6 copy-start.58
  (28 other events, 29.4 us)
Sparse Core Ops, SparseCore 0:
  275.1 94.0 reduce-scatter.4
  373.7 121.7 reduce-scatter.2
